TPU v7x, 32 devices: a whole 2x2x4 slice. The times are simulated.
32 devices in a mesh: sec: 4 (over x, core), tile: 8 (over z, y).
Axes of the slice: x: 2, y: 2, z: 4, core: 2. Of those that a mesh axis runs over, the one named last changes fastest.
Arguments:
- pixels: bfloat16 [16, 2048, 512], P('sec', 'tile'), may hold values from -6 to 6
- valid: int32 [16, 8], P('sec', 'tile'), may hold values 0 or 1
- offsets: int32 [16, 2, 64, 128], P('sec', None, 'tile'), may hold values from -64 to 63
- neighbours: int32 [16, 4, 64, 128], P('sec', None, 'tile'), may hold values from 0 to 1280, as said below
Outputs:
- ncc_maps: float32 [16, 8, 128, 128], P('sec', 'tile')
- displacement: float32 [16, 2, 64, 128], P('sec', None, 'tile')
Inputs may be any that keep to these rules, and one draw needn't show every extreme that they name: `neighbours`: slot d of a node (d = 0, 1, 2, 3 for the directions x - 1, x + 1, y - 1, y + 1) either is (10) * 128, an empty slot, or names the node's grid neighbour in that direction as local_col * 128 + row, with local_col in [0, 10): columns 1 to 8 are the tile's own, 0 and 9 the adjacent edge columns of the neighbouring tiles.
All inputs are finite; a program needn't handle non-finite values. No bound on the sum of `valid` on one device may be relied on, other than what follows from the above.
Results may differ from a plain program's by a relative error of at most 0.0085.
Values may be sent and summed in bfloat16 or wider, within the bound.
A program may use at most 64 MiB of HBM per device.

v0:
```python
import functools

import jax
import jax.numpy as jnp
import ml_dtypes
import numpy as np
from jax import lax
from jax.experimental import pallas as pl
from jax.experimental.pallas import tpu as pltpu
from jax.sharding import PartitionSpec as P

PATCH = 512
HALF = PATCH // 2
HALO = 128
SHIFTS = 128
SWEEPS = 4
EPS = 1e-06
F32 = jnp.float32
BF16 = jnp.bfloat16


def cos_sin(product):
    angles = (product % PATCH) * (2.0 * np.pi / PATCH)
    return np.cos(angles), np.sin(angles)


def tables():
    pos = np.arange(PATCH)
    freq = np.arange(HALF)
    cos, sin = cos_sin(pos[:, None] * freq[None, :])
    row_tab = np.concatenate([cos, -sin], axis=1)
    row_tab[:, HALF] = 1.0 - 2.0 * (pos % 2)
    col_tab = []
    for parity in (0, 1):
        cos, sin = cos_sin((2 * freq[:, None] + parity) * freq[None, :])
        col_tab.append(np.block([[cos, sin], [-sin, cos]]))
    shift = np.arange(SHIFTS) - SHIFTS // 2
    order = np.concatenate([2 * freq, 2 * freq + 1])
    cos, sin = cos_sin(shift[:, None] * order[None, :])
    off_tab = np.block([[cos, -sin], [sin, cos]])
    cos, sin = cos_sin(freq[:, None] * shift[None, :])
    twice = np.where(freq == 0, 1.0, 2.0)[:, None]
    map_tab = np.concatenate([cos * twice, -sin * twice], axis=0)
    return [
        np.asarray(a, np.float32).astype(ml_dtypes.bfloat16)
        for a in (row_tab, np.stack(col_tab), off_tab, map_tab)
    ]


def dot(a, b):
    return jnp.dot(a, b, preferred_element_type=F32)


def kernel(
    n_sec, n_tile,
    px, valid, off, nbr, row_hbm, col_hbm, offt_hbm, map_hbm,
    ncc_out, disp_out,
    win, offv, nbrv, row_tab, col_tab, off_tab, map_tab,
    own, mix, spec, cross, nyq, maps, energy, onehot,
    ext, wts, disp, live, inv, pull, first,
    loc_sem, halo_send, halo_recv, next_send, next_recv, ext_send, ext_recv, w_send, w_recv,
):
    sec = lax.axis_index("sec")
    tile = lax.axis_index("tile")
    secs = px.shape[0]
    width = px.shape[1]
    cols = off.shape[2]
    rows = off.shape[3]
    nxt = secs
    has_left, has_right = tile > 0, tile < n_tile - 1
    has_prev, has_next = sec > 0, sec < n_sec - 1
    sides = (
        (has_left, {"tile": tile - 1}),
        (has_right, {"tile": tile + 1}),
        (has_prev, {"sec": sec - 1}),
        (has_next, {"sec": sec + 1}),
    )

    def remote(src, dst, send, recv, to):
        return pltpu.make_async_remote_copy(
            src_ref=src, dst_ref=dst, send_sem=send, recv_sem=recv,
            device_id=to, device_id_type=pl.DeviceIdType.MESH,
        )

    barrier = pltpu.get_barrier_semaphore()
    for there, to in sides:
        @pl.when(there)
        def _(to=to):
            pl.semaphore_signal(barrier, inc=1, device_id=to, device_id_type=pl.DeviceIdType.MESH)

    local = [
        pltpu.make_async_copy(off, offv, loc_sem.at[0]),
        pltpu.make_async_copy(nbr, nbrv, loc_sem.at[1]),
        pltpu.make_async_copy(row_hbm, row_tab, loc_sem.at[2]),
        pltpu.make_async_copy(col_hbm, col_tab, loc_sem.at[3]),
        pltpu.make_async_copy(offt_hbm, off_tab, loc_sem.at[4]),
        pltpu.make_async_copy(map_hbm, map_tab, loc_sem.at[5]),
    ]
    mine = [
        pltpu.make_async_copy(px.at[s], win.at[s, pl.ds(HALO, width)], loc_sem.at[6 + s])
        for s in range(secs)
    ]
    pl.semaphore_wait(barrier, sum(there.astype(jnp.int32) for there, _ in sides))

    low = pl.ds(0, HALO)
    high = pl.ds(HALO + width, HALO)

    def halo_copy(s, side):
        if side == 0:
            return remote(px.at[s, pl.ds(0, HALO)], win.at[s, high],
                          halo_send.at[s, 0], halo_recv.at[s, 1], sides[0][1])
        return remote(px.at[s, pl.ds(width - HALO, HALO)], win.at[s, low],
                      halo_send.at[s, 1], halo_recv.at[s, 0], sides[1][1])

    def next_copy(part):
        if part == 0:
            src, dst = px.at[0], win.at[nxt, pl.ds(HALO, width)]
        else:
            place = low if part == 1 else high
            src, dst = win.at[0, place], win.at[nxt, place]
        return remote(src, dst, next_send.at[part], next_recv.at[part], sides[2][1])

    def ext_copy(side):
        if side < 2:
            src, dst = ext.at[1, 1], ext.at[1, 2 - 2 * side]
        else:
            src, dst = ext.at[1], ext.at[2 - 2 * (side - 2)]
        return remote(src, dst, ext_send.at[side], ext_recv.at[side ^ 1], sides[side][1])

    def w_copy(side):
        if side < 2:
            src, dst = wts.at[1, 1], wts.at[1, 2 - 2 * side]
        else:
            src, dst = wts.at[1], wts.at[2 - 2 * (side - 2)]
        return remote(src, dst, w_send.at[side], w_recv.at[side ^ 1], sides[side][1])

    def when(there, action):
        pl.when(there)(action)

    for s in range(secs):
        when(has_right, lambda: halo_copy(s, 1).start())
        when(has_left, lambda: halo_copy(s, 0).start())
        if s == 0:
            when(has_prev, lambda: next_copy(0).start())
    for copy in local + mine:
        copy.start()

    @pl.when(jnp.logical_not(has_left))
    def _():
        for s in range(secs):
            win[s, low] = jnp.zeros((HALO, PATCH), BF16)
        ext[1, 0] = jnp.zeros(ext.shape[2:], BF16)
        wts[1, 0] = jnp.zeros(wts.shape[2:], F32)

    @pl.when(jnp.logical_not(has_right))
    def _():
        for s in range(secs):
            win[s, high] = jnp.zeros((HALO, PATCH), BF16)
        ext[1, 2] = jnp.zeros(ext.shape[2:], BF16)
        wts[1, 2] = jnp.zeros(wts.shape[2:], F32)

    @pl.when(jnp.logical_not(has_prev))
    def _():
        ext[0] = jnp.zeros(ext.shape[1:], BF16)
        wts[0] = jnp.zeros(wts.shape[1:], F32)

    @pl.when(jnp.logical_not(has_next))
    def _():
        win[nxt] = jnp.zeros((PATCH, PATCH), BF16)
        ext[2] = jnp.zeros(ext.shape[1:], BF16)
        wts[2] = jnp.zeros(wts.shape[1:], F32)

    nyq[...] = jnp.zeros(nyq.shape, F32)

    local[0].wait()
    local[1].wait()
    limit = (cols + 2) * rows
    for s in range(secs):
        ext[1, 1, s, pl.ds(0, 2 * cols)] = offv[s].reshape(2 * cols, rows).astype(F32).astype(BF16)
        ext[1, 1, s, pl.ds(2 * cols, 4 * cols)] = jnp.where(
            nbrv[s].reshape(4 * cols, rows) < limit, F32(1.0), F32(0.0)).astype(BF16)
    when(has_left, lambda: ext_copy(0).start())
    when(has_right, lambda: ext_copy(1).start())

    local[2].wait()

    def own_rows(j):
        own[j] = dot(win[j, pl.ds(HALO, width)], row_tab[...])

    for s in range(secs):
        mine[s].wait()
        own_rows(s)

    half_win = SHIFTS // 2
    place = lax.broadcasted_iota(jnp.int32, (SHIFTS, rows), 0) - half_win

    def fill_onehot(s):
        for x in range(cols):
            hit = jnp.where(place == offv[s, 1, x:x + 1, :], F32(1.0), F32(0.0)).astype(BF16)
            onehot[s, pl.ds(0, SHIFTS), pl.ds(x * rows, rows)] = hit
            onehot[s, pl.ds(SHIFTS, SHIFTS), pl.ds(x * rows, rows)] = hit

    for s in range(secs):
        fill_onehot(s)
    for copy in local[3:]:
        copy.wait()

    lane = lax.broadcasted_iota(jnp.int32, (HALO, SHIFTS), 1)
    lane_wide = lax.broadcasted_iota(jnp.int32, (HALO, HALF), 1)

    def spectrum(j):
        pix = win[j].astype(F32)
        total = jnp.sum(jnp.sum(pix * pix, axis=0, keepdims=True), axis=1, keepdims=True)
        energy[j:j + 1, :] = jnp.broadcast_to(total * (1.0 / (PATCH * PATCH)), (1, SHIFTS))
        first_rows = dot(win[j, low], row_tab[...])
        last_rows = dot(win[j, high], row_tab[...])
        for part, (a, b) in enumerate((
            (first_rows, own[j, pl.ds(HALO, HALO)]),
            (own[j, pl.ds(0, HALO)], last_rows),
        )):
            for parity, value in enumerate((a + b, a - b)):
                mix[parity, pl.ds(part * HALO, HALO)] = value[:, :HALF].astype(BF16)
                mix[parity, pl.ds(HALF + part * HALO, HALO)] = jnp.where(
                    lane_wide == 0, F32(0.0), value[:, HALF:]).astype(BF16)
                at = (parity, pl.ds(part * HALO, HALO))
                nyq[at] = jnp.where(lane == j, value[:, HALF:HALF + 1], nyq[at])
        for parity in (0, 1):
            spec[j, parity] = dot(col_tab[parity], mix[parity])

    def cross_of(p_re, p_im, q_re, q_im):
        return (
            (p_re * q_re + p_im * q_im).astype(BF16),
            (p_re * q_im - p_im * q_re).astype(BF16),
        )

    def correlate(s):
        for parity in (0, 1):
            re, im = cross_of(
                spec[s, parity, pl.ds(0, HALF)], spec[s, parity, pl.ds(HALF, HALF)],
                spec[s + 1, parity, pl.ds(0, HALF)], spec[s + 1, parity, pl.ds(HALF, HALF)])
            cross[pl.ds(parity * HALF, HALF)] = re
            cross[pl.ds(PATCH + parity * HALF, HALF)] = im
        half = dot(off_tab[...], cross[...]).astype(BF16)
        maps[s] = dot(half[:SHIFTS], map_tab[pl.ds(0, HALF)]) + dot(
            half[SHIFTS:], map_tab[pl.ds(HALF, HALF)])

    def wait_halo(s):
        when(has_left, lambda: halo_copy(s, 1).wait_recv())
        when(has_right, lambda: halo_copy(s, 0).wait_recv())

    wait_halo(0)

    @pl.when(has_prev)
    def _():
        next_copy(1).start()
        next_copy(2).start()

    spectrum(0)
    when(has_right, lambda: ext_copy(0).wait_recv())
    when(has_left, lambda: ext_copy(1).wait_recv())
    when(has_prev, lambda: ext_copy(2).start())
    when(has_next, lambda: ext_copy(3).start())
    wait_halo(1)
    spectrum(1)
    correlate(0)

    @pl.when(has_next)
    def _():
        for part in range(3):
            next_copy(part).wait_recv()

    own_rows(nxt)
    spectrum(nxt)
    wait_halo(2)
    spectrum(2)
    correlate(1)

    when(has_prev, lambda: ext_copy(3).wait_recv())
    when(has_next, lambda: ext_copy(2).wait_recv())
    wide = 3 * cols
    for sb in range(3):
        for s in range(secs):
            at = sb * secs + s
            for tb in range(3):
                for c in range(2):
                    disp[0, at, c, pl.ds(tb * cols, cols)] = ext[
                        sb, tb, s, pl.ds(0, 2 * cols)].astype(F32)[
                            c * cols:(c + 1) * cols] * (2.0 / SHIFTS)
                for d in range(4):
                    live[at, d, pl.ds(tb * cols, cols)] = ext[
                        sb, tb, s, pl.ds(2 * cols, 4 * cols)].astype(F32)[d * cols:(d + 1) * cols]
    y = lax.broadcasted_iota(jnp.int32, (wide, rows), 1)
    x = lax.broadcasted_iota(jnp.int32, (wide, rows), 0) + (tile - 1) * cols
    inside = jnp.where(jnp.logical_and(x >= 0, x < n_tile * cols), F32(1.0), F32(0.0))
    total = n_sec * secs

    def prepare(s, carry):
        inv[s] = live[s, 0] + live[s, 1] + live[s, 2] + live[s, 3] + 1.0
        live[s, 2] = jnp.where(y > 0, live[s, 2], F32(0.0))
        live[s, 3] = jnp.where(y < rows - 1, live[s, 3], F32(0.0))
        return carry

    lax.fori_loop(1, 3 * secs - 1, prepare, 0)

    def gathered(now, s, c):
        d = disp[now, s, c]
        return (
            live[s, 0] * pltpu.roll(d, 1, 0)
            + live[s, 1] * pltpu.roll(d, wide - 1, 0)
            + live[s, 2] * pltpu.roll(d, 1, 1)
            + live[s, 3] * pltpu.roll(d, rows - 1, 1)
            + disp[now, s - 1, c]
            + disp[now, s + 1, c]
        )

    def gather_first(s, carry):
        for c in range(2):
            first[s, c] = gathered(0, s, c)
        return carry

    lax.fori_loop(1, 3 * secs - 1, gather_first, 0)

    wait_halo(3)
    spectrum(3)
    correlate(2)
    correlate(3)

    parts = []
    for parity in (0, 1):
        value = dot(col_tab[parity, :, pl.ds(0, HALF)], nyq[parity].astype(BF16))
        pair = pltpu.roll(value, SHIFTS - 1, 1)
        parts.append(cross_of(value[:HALF], value[HALF:], pair[:HALF], pair[HALF:]))
    for parity in (0, 1):
        cross[pl.ds(parity * HALF, HALF), pl.ds(0, SHIFTS)] = parts[parity][0]
        cross[pl.ds(PATCH + parity * HALF, HALF), pl.ds(0, SHIFTS)] = parts[parity][1]
    edge = dot(off_tab[pl.ds(0, SHIFTS)], cross[:, pl.ds(0, SHIFTS)]).astype(BF16).astype(F32)
    column = lax.broadcasted_iota(jnp.int32, (SHIFTS, SHIFTS), 1)
    sign = jnp.where(column % 2 == 0, F32(1.0), F32(-1.0))

    for s in range(secs):
        scale = (1.0 / float(PATCH) ** 4) / jnp.sqrt(
            energy[s:s + 1, :] * energy[s + 1:s + 2, :] + EPS)
        value = (maps[s] + edge[:, s:s + 1] * sign) * scale
        ncc_out[s, 0] = value
        upper = value.astype(BF16)
        lower = (value - upper.astype(F32)).astype(BF16)
        picked = dot(jnp.concatenate([upper, lower], axis=1), onehot[s])
        found = []
        for xi in range(cols):
            hit = place == offv[s, 0, xi:xi + 1, :]
            found.append(jnp.sum(
                jnp.where(hit, picked[:, xi * rows:(xi + 1) * rows], F32(0.0)),
                axis=0, keepdims=True))
        matched = jnp.concatenate(found, axis=0)
        wts[1, 1, s] = valid[s, 0].astype(F32) * (0.5 + 8.0 * (matched * matched))

    when(has_left, lambda: w_copy(0).start())
    when(has_right, lambda: w_copy(1).start())
    when(has_right, lambda: w_copy(0).wait_recv())
    when(has_left, lambda: w_copy(1).wait_recv())
    when(has_prev, lambda: w_copy(2).start())
    when(has_next, lambda: w_copy(3).start())
    when(has_prev, lambda: w_copy(3).wait_recv())
    when(has_next, lambda: w_copy(2).wait_recv())

    for at in range(1, 3 * secs - 1):
        w = jnp.concatenate([wts[at // secs, tb, at % secs] for tb in range(3)], axis=0)
        sid = sec * secs + (at - secs)
        one = jnp.where(jnp.logical_and(sid >= 0, sid < total), 1.0, 0.0)
        count = jnp.where(sid > 0, 1.0, 0.0) + jnp.where(sid < total - 1, 1.0, 0.0)
        share = inside * one / (inv[at] + count + w)
        inv[at] = share
        for c in range(2):
            push = w * disp[0, at, c]
            pull[at, c] = push
            disp[1, at, c] = (first[at, c] + push) * share

    now = 1
    for sweep in range(1, SWEEPS - 1):
        def relax(s, carry, now=now):
            for c in range(2):
                disp[1 - now, s, c] = (gathered(now, s, c) + pull[s, c]) * inv[s]
            return carry

        lax.fori_loop(1 + sweep, 3 * secs - 1 - sweep, relax, 0)
        now = 1 - now
    for s in range(secs):
        for c in range(2):
            at = secs + s
            value = (gathered(now, at, c) + pull[at, c]) * inv[at]
            disp_out[s, c] = value[cols:2 * cols]

    for s in range(secs):
        when(has_right, lambda: halo_copy(s, 1).wait_send())
        when(has_left, lambda: halo_copy(s, 0).wait_send())

    @pl.when(has_prev)
    def _():
        for part in range(3):
            next_copy(part).wait_send()

    for side in range(4):
        when(sides[side][0], lambda: ext_copy(side).wait_send())
        when(sides[side][0], lambda: w_copy(side).wait_send())


def shards(n_sec, n_tile, pixels, valid, offsets, neighbours):
    secs, _, cols, rows = offsets.shape
    width = pixels.shape[1]
    consts = [jnp.asarray(a) for a in tables()]
    ext_secs = 3 * secs
    any_space = pl.BlockSpec(memory_space=pl.ANY)
    vmem = pl.BlockSpec(memory_space=pltpu.VMEM)
    dma = pltpu.SemaphoreType.DMA
    return pl.pallas_call(
        functools.partial(kernel, n_sec, n_tile),
        out_shape=(
            jax.ShapeDtypeStruct((secs, 1, SHIFTS, SHIFTS), F32),
            jax.ShapeDtypeStruct((secs, 2, cols, rows), F32),
        ),
        in_specs=[any_space, pl.BlockSpec(memory_space=pltpu.SMEM)] + [any_space] * 6,
        out_specs=(vmem, vmem),
        scratch_shapes=[
            pltpu.VMEM((secs + 1, PATCH, PATCH), BF16),
            pltpu.VMEM(offsets.shape, jnp.int32),
            pltpu.VMEM(neighbours.shape, jnp.int32),
            pltpu.VMEM(consts[0].shape, BF16),
            pltpu.VMEM(consts[1].shape, BF16),
            pltpu.VMEM(consts[2].shape, BF16),
            pltpu.VMEM(consts[3].shape, BF16),
            pltpu.VMEM((secs + 1, width, PATCH), F32),
            pltpu.VMEM((2, PATCH, HALF), BF16),
            pltpu.VMEM((secs + 1, 2, PATCH, HALF), F32),
            pltpu.VMEM((2 * PATCH, HALF), BF16),
            pltpu.VMEM((2, HALF, SHIFTS), F32),
            pltpu.VMEM((secs, SHIFTS, SHIFTS), F32),
            pltpu.VMEM((8, SHIFTS), F32),
            pltpu.VMEM((secs, 2 * SHIFTS, cols * rows), BF16),
            pltpu.VMEM((3, 3, secs, 6 * cols, rows), BF16),
            pltpu.VMEM((3, 3, secs, cols, rows), F32),
            pltpu.VMEM((2, ext_secs, 2, 3 * cols, rows), F32),
            pltpu.VMEM((ext_secs, 4, 3 * cols, rows), F32),
            pltpu.VMEM((ext_secs, 3 * cols, rows), F32),
            pltpu.VMEM((ext_secs, 2, 3 * cols, rows), F32),
            pltpu.VMEM((ext_secs, 2, 3 * cols, rows), F32),
            dma((6 + secs,)),
            dma((secs, 2)), dma((secs, 2)),
            dma((3,)), dma((3,)),
            dma((4,)), dma((4,)),
            dma((4,)), dma((4,)),
        ],
        compiler_params=pltpu.CompilerParams(
            collective_id=0, has_side_effects=True, vmem_limit_bytes=48 * 2**20),
        name="align",
    )(pixels, valid, offsets, neighbours, *consts)


def solution(mesh):
    return jax.shard_map(
        functools.partial(shards, mesh.shape["sec"], mesh.shape["tile"]),
        mesh=mesh,
        in_specs=(
            P("sec", "tile", None),
            P("sec", "tile"),
            P("sec", None, "tile", None),
            P("sec", None, "tile", None),
        ),
        out_specs=(P("sec", "tile", None, None), P("sec", None, "tile", None)),
        check_vma=False,
    )
```

profile of v0, /device:TPU:13, one launch (start us, length us, event | category | flops | bytes accessed | tf_op | source)
XLA Modules:
  0.0 54.3 jit_solution(13508370742251898528)
XLA Ops:
  0.6 0.7 %copy.10.valid = s32[4,1]{1,0:T(4,128)S(1)} copy(s32[4,1]{0,1:T(1,128)} %param.9) | data formatting | bytes 32 | tf_op args[1]
  1.4 0.0 copy-start
  1.4 1.2 %copy-done = bf16[4,256,512]{2,1,0:T(8,128)(2,1)S(1)} copy-done((bf16[4,256,512]{2,1,0:T(8,128)(2,1)S(1)}, bf16[4,256,512]{2,1,0:T(8,128)(2,1)}, u32[]{:S(2)}) %copy-start) | copy-done | bytes 1048600
  2.6 0.0 copy-start.1
  2.6 1.2 %copy-done.1 = bf16[2,512,512]{2,1,0:T(8,128)(2,1)S(1)} copy-done((bf16[2,512,512]{2,1,0:T(8,128)(2,1)S(1)}, bf16[2,512,512]{2,1,0:T(8,128)(2,1)}, u32[]{:S(2)}) %copy-start.1) | copy-done | bytes 1048600
  3.8 0.0 copy-start.2
  3.8 1.0 %copy-done.2 = bf16[256,1024]{1,0:T(8,128)(2,1)S(1)} copy-done((bf16[256,1024]{1,0:T(8,128)(2,1)S(1)}, bf16[256,1024]{1,0:T(8,128)(2,1)}, u32[]{:S(2)}) %copy-start.2) | copy-done | bytes 524312
  4.9 0.0 copy-start.3
  4.9 1.0 %copy-done.3 = bf16[512,512]{1,0:T(8,128)(2,1)S(1)} copy-done((bf16[512,512]{1,0:T(8,128)(2,1)S(1)}, bf16[512,512]{1,0:T(8,128)(2,1)}, u32[]{:S(2)}) %copy-start.3) | copy-done | bytes 524312
  5.9 0.0 copy-start.4
  5.9 0.9 %copy-done.4 = bf16[512,128]{1,0:T(8,128)(2,1)S(1)} copy-done((bf16[512,128]{1,0:T(8,128)(2,1)S(1)}, bf16[512,128]{1,0:T(8,128)(2,1)}, u32[]{:S(2)}) %copy-start.4) | copy-done | bytes 131096
  6.8 0.0 copy-start.5
  6.8 0.8 %copy-done.5 = s32[4,4,8,128]{3,2,1,0:T(8,128)S(1)} copy-done((s32[4,4,8,128]{3,2,1,0:T(8,128)S(1)}, s32[4,4,8,128]{3,2,1,0:T(8,128)}, u32[]{:S(2)}) %copy-start.5) | copy-done | bytes 65560
  7.7 0.0 copy-start.6
  7.7 0.8 %copy-done.6 = s32[4,2,8,128]{3,2,1,0:T(8,128)S(1)} copy-done((s32[4,2,8,128]{3,2,1,0:T(8,128)S(1)}, s32[4,2,8,128]{3,2,1,0:T(8,128)}, u32[]{:S(2)}) %copy-start.6) | copy-done | bytes 32792
  8.4 44.6 %align.1 = (f32[4,1,128,128]{3,2,1,0:T(8,128)S(1)}, f32[4,2,8,128]{3,2,1,0:T(8,128)S(1)}) custom-call(bf16[4,256,512]{2,1,0:T(8,128)(2,1)S(1)} %copy-done, s32[4,1]{1,0:T(4,128)S(1)} %copy.10.valid, s32[4,2,8,128]{3,2,1,0:T(8,128)S(1)} %copy-done.6, s32[4,4,8,128]{3,2,1,0:T(8,128)S(1)} %copy-done.5, bf16[512,512]{1,0:T(8,128)(2,1)S(1)} %copy-done.3, ...), custom_call_target="tpu_custom_call" | custom-call | tf_op jit(solution)/shard_map/align/pallas_call | solution.py:415
  53.0 0.7 %copy.13 = f32[4,1,128,128]{3,2,1,0:T(8,128)} copy(f32[4,1,128,128]{3,2,1,0:T(8,128)S(1)} %get-tuple-element.4) | data formatting | bytes 524288
  53.7 0.6 %copy.14 = f32[4,2,8,128]{3,2,1,0:T(8,128)} copy(f32[4,2,8,128]{3,2,1,0:T(8,128)S(1)} %get-tuple-element.5) | data formatting | bytes 65536
Async XLA Ops:
  1.4 1.2 %copy-start = (bf16[4,256,512]{2,1,0:T(8,128)(2,1)S(1)}, bf16[4,256,512]{2,1,0:T(8,128)(2,1)}, u32[]{:S(2)}) copy-start(bf16[4,256,512]{2,1,0:T(8,128)(2,1)} %px.1) | copy-start | bytes 3145732
  2.6 1.2 %copy-start.1 = (bf16[2,512,512]{2,1,0:T(8,128)(2,1)S(1)}, bf16[2,512,512]{2,1,0:T(8,128)(2,1)}, u32[]{:S(2)}) copy-start(bf16[2,512,512]{2,1,0:T(8,128)(2,1)} %constant.9.clone.col_hbm) | copy-start | bytes 3145732
  3.8 1.0 %copy-start.2 = (bf16[256,1024]{1,0:T(8,128)(2,1)S(1)}, bf16[256,1024]{1,0:T(8,128)(2,1)}, u32[]{:S(2)}) copy-start(bf16[256,1024]{1,0:T(8,128)(2,1)} %constant.10.clone.offt_hbm) | copy-start | bytes 1572868
  4.9 1.0 %copy-start.3 = (bf16[512,512]{1,0:T(8,128)(2,1)S(1)}, bf16[512,512]{1,0:T(8,128)(2,1)}, u32[]{:S(2)}) copy-start(bf16[512,512]{1,0:T(8,128)(2,1)} %constant.8.clone.row_hbm) | copy-start | bytes 1572868
  5.9 0.9 %copy-start.4 = (bf16[512,128]{1,0:T(8,128)(2,1)S(1)}, bf16[512,128]{1,0:T(8,128)(2,1)}, u32[]{:S(2)}) copy-start(bf16[512,128]{1,0:T(8,128)(2,1)} %constant.11.clone.map_hbm) | copy-start | bytes 393220
  6.8 0.8 %copy-start.5 = (s32[4,4,8,128]{3,2,1,0:T(8,128)S(1)}, s32[4,4,8,128]{3,2,1,0:T(8,128)}, u32[]{:S(2)}) copy-start(s32[4,4,8,128]{3,2,1,0:T(8,128)} %nbr.1) | copy-start | bytes 196612
  7.7 0.8 %copy-start.6 = (s32[4,2,8,128]{3,2,1,0:T(8,128)S(1)}, s32[4,2,8,128]{3,2,1,0:T(8,128)}, u32[]{:S(2)}) copy-start(s32[4,2,8,128]{3,2,1,0:T(8,128)} %off.1) | copy-start | bytes 98308
where the time goes:
time: 54.8 us; the launch traced here: 54.3 us
  Pallas kernels  44.6 us (81%)
  local copies, waits for them, and re-layouts  9.09 us (17%)
  between operations  0.65 us (1%)
    pallas_call x1, Pallas kernels, shards(): pl.pallas_call(functools.partial(kernel, n_sec, n_tile), out_shape=(jax.S...  44.6 us
    unnamed x17, local copies, waits for them, and re-layouts  9.09 us

commit v1 on v0

--- a/solution.py
+++ b/solution.py
@@ -137,11 +137,13 @@
     def when(there, action):
         pl.when(there)(action)
 
-    for s in range(secs):
+    def send_halo(s):
         when(has_right, lambda: halo_copy(s, 1).start())
         when(has_left, lambda: halo_copy(s, 0).start())
-        if s == 0:
-            when(has_prev, lambda: next_copy(0).start())
+
+    send_halo(0)
+    send_halo(1)
+    when(has_prev, lambda: next_copy(0).start())
     for copy in local + mine:
         copy.start()
 
@@ -244,11 +246,40 @@
         maps[s] = dot(half[:SHIFTS], map_tab[pl.ds(0, HALF)]) + dot(
             half[SHIFTS:], map_tab[pl.ds(HALF, HALF)])
 
+    column = lax.broadcasted_iota(jnp.int32, (SHIFTS, SHIFTS), 1)
+    sign = jnp.where(column % 2 == 0, F32(1.0), F32(-1.0))
+
+    def finish(some):
+        parts = []
+        for parity in (0, 1):
+            value = dot(col_tab[parity, :, pl.ds(0, HALF)], nyq[parity].astype(BF16))
+            pair = pltpu.roll(value, SHIFTS - 1, 1)
+            parts.append(cross_of(value[:HALF], value[HALF:], pair[:HALF], pair[HALF:]))
+        both = jnp.concatenate([parts[0][0], parts[1][0], parts[0][1], parts[1][1]], axis=0)
+        edge = dot(off_tab[pl.ds(0, SHIFTS)], both).astype(BF16).astype(F32)
+        for s in some:
+            scale = (1.0 / float(PATCH) ** 4) / jnp.sqrt(
+                energy[s:s + 1, :] * energy[s + 1:s + 2, :] + EPS)
+            value = (maps[s] + edge[:, s:s + 1] * sign) * scale
+            ncc_out[s, 0] = value
+            upper = value.astype(BF16)
+            lower = (value - upper.astype(F32)).astype(BF16)
+            picked = dot(jnp.concatenate([upper, lower], axis=1), onehot[s])
+            found = []
+            for xi in range(cols):
+                hit = place == offv[s, 0, xi:xi + 1, :]
+                found.append(jnp.sum(
+                    jnp.where(hit, picked[:, xi * rows:(xi + 1) * rows], F32(0.0)),
+                    axis=0, keepdims=True))
+            matched = jnp.concatenate(found, axis=0)
+            wts[1, 1, s] = valid[0, s].astype(F32) * (0.5 + 8.0 * (matched * matched))
+
     def wait_halo(s):
         when(has_left, lambda: halo_copy(s, 1).wait_recv())
         when(has_right, lambda: halo_copy(s, 0).wait_recv())
 
     wait_halo(0)
+    send_halo(2)
 
     @pl.when(has_prev)
     def _():
@@ -261,6 +292,7 @@
     when(has_prev, lambda: ext_copy(2).start())
     when(has_next, lambda: ext_copy(3).start())
     wait_halo(1)
+    send_halo(3)
     spectrum(1)
     correlate(0)
 
@@ -274,6 +306,7 @@
     wait_halo(2)
     spectrum(2)
     correlate(1)
+    finish(range(secs - 2))
 
     when(has_prev, lambda: ext_copy(3).wait_recv())
     when(has_next, lambda: ext_copy(2).wait_recv())
@@ -325,34 +358,7 @@
     correlate(2)
     correlate(3)
 
-    parts = []
-    for parity in (0, 1):
-        value = dot(col_tab[parity, :, pl.ds(0, HALF)], nyq[parity].astype(BF16))
-        pair = pltpu.roll(value, SHIFTS - 1, 1)
-        parts.append(cross_of(value[:HALF], value[HALF:], pair[:HALF], pair[HALF:]))
-    for parity in (0, 1):
-        cross[pl.ds(parity * HALF, HALF), pl.ds(0, SHIFTS)] = parts[parity][0]
-        cross[pl.ds(PATCH + parity * HALF, HALF), pl.ds(0, SHIFTS)] = parts[parity][1]
-    edge = dot(off_tab[pl.ds(0, SHIFTS)], cross[:, pl.ds(0, SHIFTS)]).astype(BF16).astype(F32)
-    column = lax.broadcasted_iota(jnp.int32, (SHIFTS, SHIFTS), 1)
-    sign = jnp.where(column % 2 == 0, F32(1.0), F32(-1.0))
-
-    for s in range(secs):
-        scale = (1.0 / float(PATCH) ** 4) / jnp.sqrt(
-            energy[s:s + 1, :] * energy[s + 1:s + 2, :] + EPS)
-        value = (maps[s] + edge[:, s:s + 1] * sign) * scale
-        ncc_out[s, 0] = value
-        upper = value.astype(BF16)
-        lower = (value - upper.astype(F32)).astype(BF16)
-        picked = dot(jnp.concatenate([upper, lower], axis=1), onehot[s])
-        found = []
-        for xi in range(cols):
-            hit = place == offv[s, 0, xi:xi + 1, :]
-            found.append(jnp.sum(
-                jnp.where(hit, picked[:, xi * rows:(xi + 1) * rows], F32(0.0)),
-                axis=0, keepdims=True))
-        matched = jnp.concatenate(found, axis=0)
-        wts[1, 1, s] = valid[s, 0].astype(F32) * (0.5 + 8.0 * (matched * matched))
+    finish(range(secs - 2, secs))
 
     when(has_left, lambda: w_copy(0).start())
     when(has_right, lambda: w_copy(1).start())
@@ -409,7 +415,7 @@
     width = pixels.shape[1]
     consts = [jnp.asarray(a) for a in tables()]
     ext_secs = 3 * secs
-    any_space = pl.BlockSpec(memory_space=pl.ANY)
+    hbm = pl.BlockSpec(memory_space=pltpu.HBM)
     vmem = pl.BlockSpec(memory_space=pltpu.VMEM)
     dma = pltpu.SemaphoreType.DMA
     return pl.pallas_call(
@@ -418,7 +424,7 @@
             jax.ShapeDtypeStruct((secs, 1, SHIFTS, SHIFTS), F32),
             jax.ShapeDtypeStruct((secs, 2, cols, rows), F32),
         ),
-        in_specs=[any_space, pl.BlockSpec(memory_space=pltpu.SMEM)] + [any_space] * 6,
+        in_specs=[hbm, pl.BlockSpec(memory_space=pltpu.SMEM)] + [hbm] * 6,
         out_specs=(vmem, vmem),
         scratch_shapes=[
             pltpu.VMEM((secs + 1, PATCH, PATCH), BF16),
@@ -450,9 +456,9 @@
             dma((4,)), dma((4,)),
         ],
         compiler_params=pltpu.CompilerParams(
-            collective_id=0, has_side_effects=True, vmem_limit_bytes=48 * 2**20),
+            collective_id=0, has_side_effects=True, vmem_limit_bytes=63 * 2**20),
         name="align",
-    )(pixels, valid, offsets, neighbours, *consts)
+    )(pixels, valid.reshape(1, secs), offsets, neighbours, *consts)
 
 
 def solution(mesh):

time: 54.8 us -> 44.3 us (0.81)
  local copies, waits for them, and re-layouts: 9.09 us -> 2.29 us
  Pallas kernels: 44.6 us -> 41.2 us
    unnamed x17 -> x4, local copies, waits for them, and re-layouts: 9.09 us -> 2.29 us
    pallas_call x1, Pallas kernels: 44.6 us -> 41.2 us  [shards(): pl.pallas_call(functools.partial(kernel, n_sec, n_tile), out_shape=(jax.S...]
where the time goes in v1:
time: 44.3 us; the launch traced here: 44.2 us
  Pallas kernels  41.2 us (93%)
  local copies, waits for them, and re-layouts  2.29 us (5%)
  between operations  0.65 us (1%)
    pallas_call x1, Pallas kernels, shards(): pl.pallas_call(functools.partial(kernel, n_sec, n_tile), out_shape=(jax.S...  41.2 us
    unnamed x4, local copies, waits for them, and re-layouts  2.29 us

profile of v1, /device:TPU:13, one launch (start us, length us, event | category | flops | bytes accessed | tf_op | source)
XLA Modules:
  0.0 44.2 jit_solution(8973870510068777479)
XLA Ops:
  0.6 41.2 %align.1 = (f32[4,1,128,128]{3,2,1,0:T(8,128)}, f32[4,2,8,128]{3,2,1,0:T(8,128)}) custom-call(bf16[4,256,512]{2,1,0:T(8,128)(2,1)} %px.1, s32[1,4]{1,0:T(1,128)} %bitcast.1, s32[4,2,8,128]{3,2,1,0:T(8,128)} %off.1, s32[4,4,8,128]{3,2,1,0:T(8,128)} %nbr.1, bf16[512,512]{1,0:T(8,128)(2,1)} %constant.8.clone.row_hbm, ...), custom_call_target="tpu_custom_call" | custom-call | tf_op jit(solution)/shard_map/align/pallas_call | solution.py:421
  41.9 0.0 copy-start
  41.9 1.7 %copy.12 = f32[4,1,128,128]{3,2,1,0:T(8,128)} copy(f32[4,1,128,128]{3,2,1,0:T(8,128)} %get-tuple-element.4) | data formatting | bytes 524288
  43.6 0.0 copy-done
  43.6 0.6 %copy.13 = f32[4,2,8,128]{3,2,1,0:T(8,128)} copy(f32[4,2,8,128]{3,2,1,0:T(8,128)S(1)} %copy-done) | data formatting | bytes 65536
Async XLA Ops:
  41.9 1.7 %copy-start = (f32[4,2,8,128]{3,2,1,0:T(8,128)S(1)}, f32[4,2,8,128]{3,2,1,0:T(8,128)}, u32[]{:S(2)}) copy-start(f32[4,2,8,128]{3,2,1,0:T(8,128)} %get-tuple-element.5) | copy-start | bytes 98308

commit v2 on v1

--- a/solution.py
+++ b/solution.py
@@ -181,8 +181,6 @@
         ext[1, 1, s, pl.ds(0, 2 * cols)] = offv[s].reshape(2 * cols, rows).astype(F32).astype(BF16)
         ext[1, 1, s, pl.ds(2 * cols, 4 * cols)] = jnp.where(
             nbrv[s].reshape(4 * cols, rows) < limit, F32(1.0), F32(0.0)).astype(BF16)
-    when(has_left, lambda: ext_copy(0).start())
-    when(has_right, lambda: ext_copy(1).start())
 
     local[2].wait()
 
@@ -280,6 +278,8 @@
 
     wait_halo(0)
     send_halo(2)
+    when(has_left, lambda: ext_copy(0).start())
+    when(has_right, lambda: ext_copy(1).start())
 
     @pl.when(has_prev)
     def _():
@@ -287,14 +287,14 @@
         next_copy(2).start()
 
     spectrum(0)
+    wait_halo(1)
+    send_halo(3)
+    spectrum(1)
+    correlate(0)
     when(has_right, lambda: ext_copy(0).wait_recv())
     when(has_left, lambda: ext_copy(1).wait_recv())
     when(has_prev, lambda: ext_copy(2).start())
     when(has_next, lambda: ext_copy(3).start())
-    wait_halo(1)
-    send_halo(3)
-    spectrum(1)
-    correlate(0)
 
     @pl.when(has_next)
     def _():

time: 44.3 us -> 45.6 us (1.029)
  Pallas kernels: 41.2 us -> 42.5 us
    pallas_call x1, Pallas kernels: 41.2 us -> 42.5 us  [shards(): pl.pallas_call(functools.partial(kernel, n_sec, n_tile), out_shape=(jax.S...]
where the time goes in v2:
time: 45.6 us; the launch traced here: 45.4 us
  Pallas kernels  42.5 us (93%)
  local copies, waits for them, and re-layouts  2.29 us (5%)
  between operations  0.65 us (1%)
    pallas_call x1, Pallas kernels, shards(): pl.pallas_call(functools.partial(kernel, n_sec, n_tile), out_shape=(jax.S...  42.5 us
    unnamed x4, local copies, waits for them, and re-layouts  2.29 us

profile of v2, /device:TPU:13, one launch (start us, length us, event | category | flops | bytes accessed | tf_op | source)
XLA Modules:
  0.0 45.4 jit_solution(13902630057833926127)
XLA Ops:
  0.6 42.5 %align.1 = (f32[4,1,128,128]{3,2,1,0:T(8,128)}, f32[4,2,8,128]{3,2,1,0:T(8,128)}) custom-call(bf16[4,256,512]{2,1,0:T(8,128)(2,1)} %px.1, s32[1,4]{1,0:T(1,128)} %bitcast.1, s32[4,2,8,128]{3,2,1,0:T(8,128)} %off.1, s32[4,4,8,128]{3,2,1,0:T(8,128)} %nbr.1, bf16[512,512]{1,0:T(8,128)(2,1)} %constant.8.clone.row_hbm, ...), custom_call_target="tpu_custom_call" | custom-call | tf_op jit(solution)/shard_map/align/pallas_call | solution.py:421
  43.1 0.0 copy-start
  43.1 1.7 %copy.12 = f32[4,1,128,128]{3,2,1,0:T(8,128)} copy(f32[4,1,128,128]{3,2,1,0:T(8,128)} %get-tuple-element.4) | data formatting | bytes 524288
  44.8 0.0 copy-done
  44.8 0.6 %copy.13 = f32[4,2,8,128]{3,2,1,0:T(8,128)} copy(f32[4,2,8,128]{3,2,1,0:T(8,128)S(1)} %copy-done) | data formatting | bytes 65536
Async XLA Ops:
  43.1 1.7 %copy-start = (f32[4,2,8,128]{3,2,1,0:T(8,128)S(1)}, f32[4,2,8,128]{3,2,1,0:T(8,128)}, u32[]{:S(2)}) copy-start(f32[4,2,8,128]{3,2,1,0:T(8,128)} %get-tuple-element.5) | copy-start | bytes 98308
